TPU v7x, 32 devices: a whole 2x2x4 slice. The times are simulated.
32 devices in a mesh: dp: 8 (over y, x, core), mp: 4 (over z).
Axes of the slice: x: 2, y: 2, z: 4, core: 2. Of those that a mesh axis runs over, the one named last changes fastest.
Arguments:
- response_query: bfloat16 [384, 8, 6144], P('dp', None, 'mp'), may hold values from -80 to 80, as said below
- response_keys: bfloat16 [2, 384, 8, 768], P(None, 'dp'), may hold values from -8 to 8
- prompt_cache: bfloat16 [2, 8, 1024, 768], P(None, 'dp'), may hold values from -6 to 6
- lengths: int32 [384], P('dp'), may hold values from 1 to 8, as said below
- owners: int32 [384], P('dp'), may hold values from 0 to 7, as said below
- pairing: int32 [384], replicated, may hold values from 0 to 383, each once
- residual: bfloat16 [384, 8192], P(None, 'dp'), may hold values from -90 to 90
- output_weight: bfloat16 [6144, 8192], P('mp', 'dp'), may hold values from -0.3125 to 0.3125
- norm_gain: float32 [8192], P('dp'), may hold values from 0.1 to 1.9
- reward_head: float32 [8192], P('dp'), may hold values from -0.0625 to 0.0625
Outputs:
- attention_rows: bfloat16 [384, 8, 6144], P('dp', None, 'mp')
- rewards: float32 [384], replicated
- pair_loss: float32 [], replicated
- weight_gradient: float32 [6144, 8192], P('mp', 'dp')
- head_gradient: float32 [8192], P('dp')
- pooled_gradient: float32 [384, 6144], P('dp', 'mp')
Inputs may be any that keep to these rules, and one draw needn't show every extreme that they name: `response_query`: drawn jointly with response_keys. `lengths`: every dp index holds a response of length 8. The responses of one dp index spread over owners as evenly as possible: each owner receives at most 6 of them, and some owner receives exactly 6.
All inputs are finite; a program needn't handle non-finite values.
Results may differ from a plain program's by a relative error of at most 0.0056.
Values may be sent and summed in bfloat16 or wider, within the bound.
A program may use at most 64 MiB of HBM per device.

v0:
```python
import math
import jax
import jax.numpy as jnp
from jax import lax
from jax.sharding import PartitionSpec as P

D = 8192
HD = 128
Q_HEADS = 48
KV_HEADS = 6
EPSILON = 1e-05


def bradley_terry(rewards, pairing):
    chosen = pairing[0::2]
    rejected = pairing[1::2]
    margin = rewards[chosen] - rewards[rejected]
    loss_value = jnp.mean(jax.nn.softplus(-margin))
    slope = -jax.nn.sigmoid(-margin) / margin.shape[0]
    reward_slope = jnp.zeros_like(rewards).at[chosen].add(slope).at[rejected].add(-slope)
    return (loss_value, reward_slope)


def shards(
    response_query,
    response_keys,
    prompt_cache,
    lengths,
    owners,
    pairing,
    residual,
    output_weight,
    norm_gain,
    reward_head,
):
    groups = lax.axis_size("dp")
    model_rank = lax.axis_index("mp")
    held_count = response_query.shape[0]
    slot_count = response_query.shape[1]
    head_width = response_query.shape[2]
    local_heads = head_width // HD
    group_size = Q_HEADS // KV_HEADS
    per_owner = (held_count + groups - 1) // groups
    if group_size % local_heads == 0:
        window = 1
    elif local_heads % group_size == 0:
        window = local_heads // group_size
    else:
        window = min(KV_HEADS, (local_heads - 1) // group_size + 2)
    first_head = jnp.minimum(model_rank * local_heads // group_size, KV_HEADS - window)
    head_slot = (model_rank * local_heads + jnp.arange(local_heads)) // group_size - first_head
    score_scale = 1.0 / math.sqrt(HD)
    own_window = lax.dynamic_slice_in_dim(response_keys, first_head * HD, window * HD, 3)
    spread = own_window.reshape(2, held_count, slot_count, window, HD)
    picked = jnp.take(spread, head_slot, axis=3).reshape(
        2, held_count, slot_count, local_heads * HD
    )
    key_pick = jnp.arange(local_heads)
    outgoing_keys = jnp.concatenate([picked[0], picked[1]], axis=-1)
    positions = jnp.arange(held_count)
    earlier = (owners[None, :] == owners[:, None]) & (positions[None, :] < positions[:, None])
    target = owners * per_owner + jnp.sum(earlier, axis=1)
    capacity = groups * per_owner
    query_buffer = (
        jnp.zeros((capacity, slot_count, head_width), jnp.bfloat16).at[target].set(response_query)
    )
    query_buffer = query_buffer.reshape(groups, per_owner, slot_count, head_width)
    key_buffer = (
        jnp.zeros((capacity, slot_count, 2 * local_heads * HD), jnp.bfloat16)
        .at[target]
        .set(outgoing_keys)
    )
    key_buffer = key_buffer.reshape(groups, per_owner, slot_count, 2 * local_heads * HD)
    length_buffer = (
        jnp.zeros((capacity,), jnp.int32).at[target].set(lengths).reshape(groups, per_owner)
    )
    prefix = lax.dynamic_slice_in_dim(prompt_cache[:, 0], first_head * HD, window * HD, 2)
    query_in = lax.all_to_all(query_buffer, "dp", split_axis=0, concat_axis=0, tiled=True)
    keys_in = lax.all_to_all(key_buffer, "dp", split_axis=0, concat_axis=0, tiled=True)
    length_in = lax.all_to_all(length_buffer, "dp", split_axis=0, concat_axis=0, tiled=True)
    sources = query_in.shape[0]
    item_count = query_in.shape[1]
    blocks = sources * item_count
    row_count = blocks * slot_count
    queries = query_in.reshape(blocks, slot_count, local_heads, HD)
    own_keys = keys_in.reshape(blocks, slot_count, 2, local_heads, HD)
    live_length = length_in.reshape(blocks)
    offsets = jnp.arange(slot_count)
    allowed = (offsets[None, None, :] <= offsets[None, :, None]) & (
        offsets[None, None, :] < live_length[:, None, None]
    )
    valid_rows = offsets[None, :] < live_length[:, None]

    def one_head(head_index):
        query_head = lax.dynamic_index_in_dim(queries, head_index, 2, keepdims=False)
        self_pair = lax.dynamic_index_in_dim(own_keys, key_pick[head_index], 3, keepdims=False)
        cache_pair = lax.dynamic_slice_in_dim(prefix, head_slot[head_index] * HD, HD, 2)
        flat_query = query_head.reshape(row_count, HD)
        far_scores = (
            lax.dot_general(
                flat_query,
                cache_pair[0],
                (((1,), (1,)), ((), ())),
                preferred_element_type=jnp.float32,
            )
            * score_scale
        )
        near_scores = (
            jnp.einsum(
                "bth,bsh->bts", query_head, self_pair[:, :, 0], preferred_element_type=jnp.float32
            )
            * score_scale
        )
        near_scores = jnp.where(allowed, near_scores, -jnp.inf)
        row_top = jnp.maximum(
            jnp.max(far_scores, axis=1).reshape(blocks, slot_count), jnp.max(near_scores, axis=2)
        )
        far_weight = jnp.exp(far_scores - row_top.reshape(row_count, 1))
        near_weight = jnp.exp(near_scores - row_top[:, :, None])
        weight_total = jnp.sum(far_weight, axis=1).reshape(blocks, slot_count) + jnp.sum(
            near_weight, axis=2
        )
        output = jnp.dot(
            far_weight.astype(jnp.bfloat16), cache_pair[1], preferred_element_type=jnp.float32
        ).reshape(blocks, slot_count, HD)
        output = output + jnp.einsum(
            "bts,bsh->bth",
            near_weight.astype(jnp.bfloat16),
            self_pair[:, :, 1],
            preferred_element_type=jnp.float32,
        )
        output = output / weight_total[:, :, None]
        return jnp.where(valid_rows[:, :, None], output, 0.0).astype(jnp.bfloat16)

    heads_out = lax.map(one_head, jnp.arange(local_heads))
    result = jnp.transpose(heads_out, (1, 2, 0, 3)).reshape(
        sources, item_count, slot_count, head_width
    )
    returned = lax.all_to_all(result, "dp", split_axis=0, concat_axis=0, tiled=True)
    attention_rows = returned.reshape(capacity, slot_count, head_width)[target]
    pooled_local = attention_rows[positions, lengths - 1]
    pooled_all = lax.all_gather(pooled_local, "dp", axis=0, tiled=True)
    partial_mix = jnp.dot(pooled_all, output_weight, preferred_element_type=jnp.float32)
    scaled_head = norm_gain * reward_head
    combined = lax.psum(partial_mix, "mp") + residual.astype(jnp.float32)
    square_sum = jnp.sum(combined * combined, axis=1)
    signal = jnp.sum(combined * scaled_head[None, :], axis=1)
    square_sum, signal = lax.psum((square_sum, signal), "dp")
    inverse = lax.rsqrt(square_sum / D + EPSILON)
    rewards = inverse * signal
    pair_loss, reward_slope = bradley_terry(rewards, pairing)
    direct_term = reward_slope * inverse
    norm_term = reward_slope * inverse * inverse * inverse * signal / D
    upstream = direct_term[:, None] * scaled_head[None, :] - norm_term[:, None] * combined
    head_gradient = jnp.sum(direct_term[:, None] * combined * norm_gain[None, :], axis=0)
    upstream_half = upstream.astype(jnp.bfloat16)
    weight_gradient = lax.dot_general(
        pooled_all, upstream_half, (((0,), (0,)), ((), ())), preferred_element_type=jnp.float32
    )
    pooled_gradient = lax.psum_scatter(
        lax.dot_general(
            upstream_half,
            output_weight,
            (((1,), (1,)), ((), ())),
            preferred_element_type=jnp.float32,
        ),
        "dp",
        scatter_dimension=0,
        tiled=True,
    )
    return (attention_rows, rewards, pair_loss, weight_gradient, head_gradient, pooled_gradient)


def solution(mesh):
    placed = (
        P("dp", None, "mp"),
        P(None, "dp", None, None),
        P(None, "dp", None, None),
        P("dp"),
        P("dp"),
        P(),
        P(None, "dp"),
        P("mp", "dp"),
        P("dp"),
        P("dp"),
    )
    return jax.shard_map(
        shards,
        mesh=mesh,
        in_specs=placed,
        out_specs=(P("dp", None, "mp"), P(), P(), P("mp", "dp"), P("dp"), P("dp", "mp")),
        check_vma=False,
    )
```

profile of v0, /device:TPU:0, one launch (start us, length us, event | category | flops | bytes accessed | tf_op | source)
XLA Modules:
  0.0 529.6 jit_solution(9194661605754231046)
XLA Ops:
  10.4 5.2 all-to-all-start
  18.1 3.6 gather_fusion
  21.8 3.4 select_bitcast_fusion
  26.2 7.2 %scatter_fusion = bf16[48,8,1536]{2,1,0:T(8,128)(2,1)} fusion(bf16[48,8,1536]{2,1,0:T(8,128)(2,1)} %broadcast_in_dim.88, s32[48]{0:T(128)S(1)} %compare_select_fusion.6, bf16[48,8,1536]{2,1,0:T(8,128)(2,1)} %param.12), kind=kCustom, calls=%fused_computation.6 | custom fusion | bytes 3539136 | tf_op jit(solution)/shard_map/scatter | solution.py:65
  33.4 4.2 all-to-all-start.1
  43.2 8.2 %scatter_fusion.1 = bf16[48,8,3072]{2,1,0:T(8,128)(2,1)} fusion(bf16[48,8,3072]{2,1,0:T(8,128)(2,1)} %broadcast_in_dim.89, s32[48]{0:T(128)S(1)} %compare_select_fusion.6, bf16[48,8,3072]{2,1,0:T(8,128)(2,1)} %pad_maximum_fusion), kind=kCustom, calls=%fused_computation.7 | custom fusion | bytes 7078080 | tf_op jit(solution)/shard_map/scatter | solution.py:71
  51.4 3.1 all-to-all-done.1
  54.5 4.4 all-to-all-start.2
  58.9 2.7 dynamic-slice_bitcast_fusion.4
  62.9 25.4 %all-to-all-done.2 = bf16[8,6,8,3072]{3,2,1,0:T(8,128)(2,1)} async-done(((bf16[8,6,8,3072]{3,2,1,0:T(8,128)(2,1)}), bf16[8,6,8,3072]{3,2,1,0:T(8,128)(2,1)}, u32[]{:S(2)}, u32[]{:S(2)}) %all-to-all-start.2) | async-done | bytes 2359328 | tf_op jit(solution)/shard_map/all_to_all | solution.py:79
  88.9 239.0 %while.13 = (s32[]{:T(128)}, bf16[12,48,8,128]{3,2,0,1:T(8,128)(2,1)}, s32[12]{0:T(128)}, bf16[48,8,12,128]{3,1,2,0:T(8,128)(2,1)}, s32[12]{0:T(128)}, /*index=5...) while((s32[]{:T(128)}, ...), condition=%wide.region_9.10_spmd.clone.clone, body=%wide.region_4.9_spmd.clone.clone.sunk | while | flops 205486080 | bytes 6827307 | solution.py:135
  133.8 2.5 fusion.67
  327.9 4.4 all-to-all-start.3
  332.4 16.7 %all-to-all-done.3 = bf16[8,6,8,1536]{3,2,1,0:T(8,128)(2,1)} async-done(((bf16[8,6,8,1536]{3,2,1,0:T(8,128)(2,1)}), bf16[8,6,8,1536]{3,2,1,0:T(8,128)(2,1)}, u32[]{:S(2)}, u32[]{:S(2)}) %all-to-all-start.3) | async-done | bytes 1179680 | tf_op jit(solution)/shard_map/all_to_all | solution.py:139
  349.2 3.0 gather_fusion.1
  352.1 3.2 gather_fusion.2
  355.4 23.6 %all-gather.2.cloned.1.call-done = bf16[384,1536]{1,0:T(8,128)(2,1)} async-done(((bf16[48,1536]{1,0:T(8,128)(2,1)}), bf16[384,1536]{1,0:T(8,128)(2,1)}) %all-gather.2.cloned.1.call-update) | async-done | bytes 1179664 | tf_op jit(solution)/shard_map/all_gather | solution.py:142
  378.9 3.8 fusion.44
  383.9 68.1 %all-reduce.3.cloned.1.call-done = f32[384,1024]{1,0:T(8,128)} async-done(((f32[384,1024]{1,0:T(8,128)}), f32[384,1024]{1,0:T(8,128)}) %all-reduce.3.cloned.1.call-update) | async-done | bytes 1572880 | tf_op jit(solution)/shard_map/psum | solution.py:145
  454.0 12.5 %all-reduce = (f32[384]{0:T(512)S(1)}, f32[384]{0:T(512)S(1)}) all-reduce(f32[384]{0:T(512)S(1)} %get-tuple-element.190, f32[384]{0:T(512)S(1)} %get-tuple-element.189), channel_id=1, replica_groups=mesh['dp'=8,'mp'=4] {'dp'}, use_global_device_ids=true, to_apply=%region_14.15 | all-reduce | flops 768 | bytes 6144 | tf_op jit(solution)/shard_map/psum | solution.py:148
  474.4 2.7 multiply_reduce_fusion
  477.9 2.9 fusion.46
  481.5 6.0 %fusion.45 = f32[1536,1024]{1,0:T(8,128)} fusion(bf16[384,1536]{1,0:T(8,128)(2,1)} %all-gather.2.cloned.1.call-done, bf16[384,1024]{1,0:T(8,128)(2,1)} %copy-done.3), kind=kOutput, calls=%fused_computation.102 | convolution fusion | flops 1207959552 | bytes 8257536 | tf_op jit(solution)/shard_map/dot_general | solution.py:157
  487.5 34.5 %reduce-scatter.2.cloned.1.call-done = f32[48,1536]{1,0:T(8,128)} async-done(((f32[384,1536]{1,0:T(8,128)}), f32[48,1536]{1,0:T(8,128)}) %reduce-scatter.2.cloned.1.call-update) | async-done | bytes 294928 | tf_op jit(solution)/shard_map/reduce_scatter | solution.py:160
  (373 shorter events, 207.2 us)
Async XLA Ops:
  7.2 371.8 %copy-start = (bf16[1536,1024]{1,0:T(8,128)(2,1)S(1)}, bf16[1536,1024]{1,0:T(8,128)(2,1)}, u32[]{:S(2)}) copy-start(bf16[1536,1024]{1,0:T(8,128)(2,1)} %param.19) | copy-start | bytes 9437188
  8.9 34.3 %copy-start.5 = (s32[48]{0:T(128)}, s32[48]{0:T(128)S(1)}, u32[]{:S(2)}) copy-start(s32[48]{0:T(128)S(1)} %compare_select_fusion.6) | copy-start | bytes 580
  10.4 23.0 %all-to-all-start = ((s32[8,1,6]{2,1,0:T(1,128)}), s32[8,1,6]{2,1,0:T(1,128)S(1)}, u32[]{:S(2)}, u32[]{:S(2)}) async-start(s32[8,1,6]{2,1,0:T(1,128)} %bitcast.10), calls=%async_computation | async-start | bytes 8192 | tf_op jit(solution)/shard_map/all_to_all | solution.py:80
  33.4 21.1 %all-to-all-start.1 = ((bf16[8,6,8,1536]{3,2,1,0:T(8,128)(2,1)}), bf16[8,6,8,1536]{3,2,1,0:T(8,128)(2,1)}, u32[]{:S(2)}, u32[]{:S(2)}) async-start(bf16[8,6,8,1536]{3,2,1,0:T(8,128)(2,1)} %bitcast.101), calls=%async_computation.1 | async-start | bytes 2359296 | tf_op jit(solution)/shard_map/all_to_all | solution.py:78
  54.5 33.8 %all-to-all-start.2 = ((bf16[8,6,8,3072]{3,2,1,0:T(8,128)(2,1)}), bf16[8,6,8,3072]{3,2,1,0:T(8,128)(2,1)}, u32[]{:S(2)}, u32[]{:S(2)}) async-start(bf16[8,6,8,3072]{3,2,1,0:T(8,128)(2,1)} %bitcast.100), calls=%async_computation.2 | async-start | bytes 4718592 | tf_op jit(solution)/shard_map/all_to_all | solution.py:79
  102.5 3.2 copy-start.2
  122.4 3.2 copy-start.2
  142.3 3.2 copy-start.2
  162.2 3.2 copy-start.2
  182.2 3.2 copy-start.2
  202.1 3.2 copy-start.2
  222.0 3.2 copy-start.2
  241.9 3.2 copy-start.2
  261.8 3.2 copy-start.2
  281.8 3.2 copy-start.2
  301.7 3.2 copy-start.2
  321.6 3.2 copy-start.2
  327.9 4.4 copy-start.6
  327.9 4.5 copy-start.9
  327.9 21.2 %all-to-all-start.3 = ((bf16[8,6,8,1536]{3,2,1,0:T(8,128)(2,1)}), bf16[8,6,8,1536]{3,2,1,0:T(8,128)(2,1)}, u32[]{:S(2)}, u32[]{:S(2)}) async-start(bf16[8,6,8,1536]{3,2,1,0:T(8,128)(2,1)} %bitcast.12), calls=%async_computation.3 | async-start | bytes 2359296 | tf_op jit(solution)/shard_map/all_to_all | solution.py:139
  332.3 46.6 %all-gather.2.cloned.1.call-start = ((), (), s32[]{:S(2)}) async-start(), calls=%async_computation.5 | async-start | bytes 1327104 | tf_op jit(solution)/shard_map/all_gather | solution.py:142
  355.3 96.7 %all-reduce.3.cloned.1.call-start = ((), (), s32[]{:S(2)}) async-start(), calls=%async_computation.6 | async-start | bytes 3145728 | tf_op jit(solution)/shard_map/psum | solution.py:145
  382.8 139.2 %reduce-scatter.2.cloned.1.call-start = ((), (), s32[]{:S(2)}) async-start(), calls=%async_computation.7 | async-start | bytes 2654208 | tf_op jit(solution)/shard_map/reduce_scatter | solution.py:160
  466.5 7.8 %copy-start.1 = (f32[384]{0:T(512)}, f32[384]{0:T(512)S(1)}, u32[]{:S(2)}) copy-start(f32[384]{0:T(512)S(1)} %fusion.33) | copy-start | bytes 4612
  (4 other events, 3.8 us)
Sparse Core Ops, SparseCore 0:
  355.4 23.4 all-gather.1
  382.9 69.0 all-reduce.2
  480.9 40.9 reduce-scatter.1
where the time goes:
time: 534 us; the launch traced here: 530 us
  waiting for transfers between devices  171 us (32%)
  local copies, waits for them, and re-layouts  116 us (22%)
  matrix products  88.1 us (16%)
  loops' own time  55.3 us (10%)
  other arithmetic  52 us (10%)
  starting transfers between devices  18.3 us (3%)
  between operations  15.7 us (3%)
  blocking collectives  12.5 us (2%)
    psum x1, waiting for transfers between devices, shards(): combined = lax.psum(partial_mix, 'mp') + residual.astype(jnp.float32)  68.1 us
    another operation x1, loops' own time, shards(): heads_out = lax.map(one_head, jnp.arange(local_heads))  55.3 us
    reduce_scatter x1, waiting for transfers between devices, shards(): lax.psum_scatter(lax.dot_general(upstream_half, output_weight, (((1,), (1...  34.5 us
    dot_general x12, matrix products, one_head(): lax.dot_general(flat_query, cache_pair[0], (((1,), (1,)), ((), ())), pref...  30.3 us
    all_to_all x1, waiting for transfers between devices, shards(): lax.all_to_all(key_buffer, 'dp', split_axis=0, concat_axis=0, tiled=True)  25.4 us
    all_gather x1, waiting for transfers between devices, shards(): pooled_all = lax.all_gather(pooled_local, 'dp', axis=0, tiled=True)  23.6 us
    dot_general x12, matrix products, one_head(): jnp.dot(far_weight.astype(jnp.bfloat16), cache_pair[1], preferred_element...  22.2 us
    reduce_sum x12, other arithmetic, one_head(): jnp.sum(far_weight, axis=1).reshape(blocks, slot_count)  21.4 us
  transfers between devices with their start and end apart: 7, of which 6 were waited for; matrix products, arithmetic and copies ran while one was open for 8% of the time, Pallas kernels for 0%

commit v1 on v0

--- a/solution.py
+++ b/solution.py
@@ -3,6 +3,7 @@
 import jax.numpy as jnp
 from jax import lax
 from jax.sharding import PartitionSpec as P
+from jax.lax import all_gather
 
 D = 8192
 HD = 128
@@ -142,7 +143,7 @@
     pooled_all = lax.all_gather(pooled_local, "dp", axis=0, tiled=True)
     partial_mix = jnp.dot(pooled_all, output_weight, preferred_element_type=jnp.float32)
     scaled_head = norm_gain * reward_head
-    combined = lax.psum(partial_mix, "mp") + residual.astype(jnp.float32)
+    combined = jnp.sum(all_gather(partial_mix, "mp"), axis=0) + residual.astype(jnp.float32)
     square_sum = jnp.sum(combined * combined, axis=1)
     signal = jnp.sum(combined * scaled_head[None, :], axis=1)
     square_sum, signal = lax.psum((square_sum, signal), "dp")

time: 534 us -> 584 us (1.094)
  waiting for transfers between devices: 171 us -> 215 us
    all_gather x0 -> x1, waiting for transfers between devices: none -> 114 us  [shards(): all_gather(partial_mix, 'mp')]
    psum x1 -> x0, waiting for transfers between devices: 68.1 us -> none  [shards(): combined = lax.psum(partial_mix, 'mp') + residual.astype(jnp.float32)]
  transfers between devices with their start and end apart: 7 -> 7, of which waited for: 6 -> 6; matrix products, arithmetic and copies ran while one was open for 8% -> 7% of each run, Pallas kernels for 0% -> 0%
where the time goes in v1:
time: 584 us; the launch traced here: 580 us
  waiting for transfers between devices  215 us (37%)
  local copies, waits for them, and re-layouts  116 us (20%)
  matrix products  88.3 us (15%)
  other arithmetic  56.8 us (10%)
  loops' own time  55.3 us (9%)
  starting transfers between devices  18.3 us (3%)
  between operations  15.7 us (3%)
  blocking collectives  13.8 us (2%)
    all_gather x1, waiting for transfers between devices, shards(): all_gather(partial_mix, 'mp')  114 us
    another operation x1, loops' own time, shards(): heads_out = lax.map(one_head, jnp.arange(local_heads))  55.3 us
    reduce_scatter x1, waiting for transfers between devices, shards(): lax.psum_scatter(lax.dot_general(upstream_half, output_weight, (((1,), (1...  32.1 us
    dot_general x12, matrix products, one_head(): lax.dot_general(flat_query, cache_pair[0], (((1,), (1,)), ((), ())), pref...  30.3 us
    all_to_all x1, waiting for transfers between devices, shards(): lax.all_to_all(key_buffer, 'dp', split_axis=0, concat_axis=0, tiled=True)  25.4 us
    all_gather x1, waiting for transfers between devices, shards(): pooled_all = lax.all_gather(pooled_local, 'dp', axis=0, tiled=True)  23.6 us
    dot_general x12, matrix products, one_head(): jnp.dot(far_weight.astype(jnp.bfloat16), cache_pair[1], preferred_element...  22.2 us
    reduce_sum x12, other arithmetic, one_head(): jnp.sum(far_weight, axis=1).reshape(blocks, slot_count)  21.4 us
  transfers between devices with their start and end apart: 7, of which 6 were waited for; matrix products, arithmetic and copies ran while one was open for 7% of the time, Pallas kernels for 0%

profile of v1, /device:TPU:0, one launch (start us, length us, event | category | flops | bytes accessed | tf_op | source)
XLA Modules:
  0.0 579.8 jit_solution(12845692437926013171)
XLA Ops:
  10.4 5.2 all-to-all-start
  18.1 3.6 gather_fusion
  21.8 3.4 select_bitcast_fusion
  26.2 7.2 %scatter_fusion = bf16[48,8,1536]{2,1,0:T(8,128)(2,1)} fusion(bf16[48,8,1536]{2,1,0:T(8,128)(2,1)} %broadcast_in_dim.88, s32[48]{0:T(128)S(1)} %compare_select_fusion.6, bf16[48,8,1536]{2,1,0:T(8,128)(2,1)} %param.12), kind=kCustom, calls=%fused_computation.6 | custom fusion | bytes 3539136 | tf_op jit(solution)/shard_map/scatter | solution.py:66
  33.4 4.2 all-to-all-start.1
  43.2 8.2 %scatter_fusion.1 = bf16[48,8,3072]{2,1,0:T(8,128)(2,1)} fusion(bf16[48,8,3072]{2,1,0:T(8,128)(2,1)} %broadcast_in_dim.89, s32[48]{0:T(128)S(1)} %compare_select_fusion.6, bf16[48,8,3072]{2,1,0:T(8,128)(2,1)} %pad_maximum_fusion), kind=kCustom, calls=%fused_computation.7 | custom fusion | bytes 7078080 | tf_op jit(solution)/shard_map/scatter | solution.py:72
  51.4 3.1 all-to-all-done.1
  54.5 4.4 all-to-all-start.2
  58.9 2.7 dynamic-slice_bitcast_fusion.4
  62.9 25.4 %all-to-all-done.2 = bf16[8,6,8,3072]{3,2,1,0:T(8,128)(2,1)} async-done(((bf16[8,6,8,3072]{3,2,1,0:T(8,128)(2,1)}), bf16[8,6,8,3072]{3,2,1,0:T(8,128)(2,1)}, u32[]{:S(2)}, u32[]{:S(2)}) %all-to-all-start.2) | async-done | bytes 2359328 | tf_op jit(solution)/shard_map/all_to_all | solution.py:80
  88.9 239.0 %while.13 = (s32[]{:T(128)}, bf16[12,48,8,128]{3,2,0,1:T(8,128)(2,1)}, s32[12]{0:T(128)}, bf16[48,8,12,128]{3,1,2,0:T(8,128)(2,1)}, s32[12]{0:T(128)}, /*index=5...) while((s32[]{:T(128)}, ...), condition=%wide.region_9.10_spmd.clone.clone, body=%wide.region_4.9_spmd.clone.clone.sunk | while | flops 205486080 | bytes 6827307 | solution.py:136
  327.9 4.4 all-to-all-start.3
  332.4 16.7 %all-to-all-done.3 = bf16[8,6,8,1536]{3,2,1,0:T(8,128)(2,1)} async-done(((bf16[8,6,8,1536]{3,2,1,0:T(8,128)(2,1)}), bf16[8,6,8,1536]{3,2,1,0:T(8,128)(2,1)}, u32[]{:S(2)}, u32[]{:S(2)}) %all-to-all-start.3) | async-done | bytes 1179680 | tf_op jit(solution)/shard_map/all_to_all | solution.py:140
  349.2 3.0 gather_fusion.1
  352.1 3.2 gather_fusion.2
  355.4 23.6 %all-gather.4.cloned.1.call-done = bf16[384,1536]{1,0:T(8,128)(2,1)} async-done(((bf16[48,1536]{1,0:T(8,128)(2,1)}), bf16[384,1536]{1,0:T(8,128)(2,1)}) %all-gather.4.cloned.1.call-update) | async-done | bytes 1179664 | tf_op jit(solution)/shard_map/all_gather | solution.py:143
  378.9 3.8 fusion.44
  383.9 114.3 %all-gather.6.cloned.1.call-done = f32[1536,1024]{1,0:T(8,128)} async-done(((f32[384,1024]{1,0:T(8,128)}), f32[1536,1024]{1,0:T(8,128)}) %all-gather.6.cloned.1.call-update) | async-done | bytes 6291472 | tf_op jit(solution)/shard_map/all_gather | solution.py:146
  498.3 4.8 reduce_sum.75
  505.0 13.8 %all-reduce = (f32[384]{0:T(512)S(1)}, f32[384]{0:T(512)S(1)}) all-reduce(f32[384]{0:T(512)S(1)} %get-tuple-element.190, f32[384]{0:T(512)S(1)} %get-tuple-element.189), channel_id=1, replica_groups=mesh['dp'=8,'mp'=4] {'dp'}, use_global_device_ids=true, to_apply=%region_14.15 | all-reduce | flops 768 | bytes 6144 | tf_op jit(solution)/shard_map/psum | solution.py:149
  526.7 2.7 multiply_reduce_fusion
  530.3 2.9 fusion.46
  533.8 6.2 %fusion.45 = f32[1536,1024]{1,0:T(8,128)} fusion(bf16[384,1536]{1,0:T(8,128)(2,1)} %all-gather.4.cloned.1.call-done, bf16[384,1024]{1,0:T(8,128)(2,1)} %copy-done.3), kind=kOutput, calls=%fused_computation.102 | convolution fusion | flops 1207959552 | bytes 8257536 | tf_op jit(solution)/shard_map/dot_general | solution.py:158
  540.0 32.1 %reduce-scatter.2.cloned.1.call-done = f32[48,1536]{1,0:T(8,128)} async-done(((f32[384,1536]{1,0:T(8,128)}), f32[48,1536]{1,0:T(8,128)}) %reduce-scatter.2.cloned.1.call-update) | async-done | bytes 294928 | tf_op jit(solution)/shard_map/reduce_scatter | solution.py:161
  (374 shorter events, 209.8 us)
Async XLA Ops:
  7.2 371.8 %copy-start = (bf16[1536,1024]{1,0:T(8,128)(2,1)S(1)}, bf16[1536,1024]{1,0:T(8,128)(2,1)}, u32[]{:S(2)}) copy-start(bf16[1536,1024]{1,0:T(8,128)(2,1)} %param.19) | copy-start | bytes 9437188
  8.9 34.3 %copy-start.5 = (s32[48]{0:T(128)}, s32[48]{0:T(128)S(1)}, u32[]{:S(2)}) copy-start(s32[48]{0:T(128)S(1)} %compare_select_fusion.6) | copy-start | bytes 580
  10.4 23.0 %all-to-all-start = ((s32[8,1,6]{2,1,0:T(1,128)}), s32[8,1,6]{2,1,0:T(1,128)S(1)}, u32[]{:S(2)}, u32[]{:S(2)}) async-start(s32[8,1,6]{2,1,0:T(1,128)} %bitcast.10), calls=%async_computation | async-start | bytes 8192 | tf_op jit(solution)/shard_map/all_to_all | solution.py:81
  33.4 21.1 %all-to-all-start.1 = ((bf16[8,6,8,1536]{3,2,1,0:T(8,128)(2,1)}), bf16[8,6,8,1536]{3,2,1,0:T(8,128)(2,1)}, u32[]{:S(2)}, u32[]{:S(2)}) async-start(bf16[8,6,8,1536]{3,2,1,0:T(8,128)(2,1)} %bitcast.102), calls=%async_computation.1 | async-start | bytes 2359296 | tf_op jit(solution)/shard_map/all_to_all | solution.py:79
  54.5 33.8 %all-to-all-start.2 = ((bf16[8,6,8,3072]{3,2,1,0:T(8,128)(2,1)}), bf16[8,6,8,3072]{3,2,1,0:T(8,128)(2,1)}, u32[]{:S(2)}, u32[]{:S(2)}) async-start(bf16[8,6,8,3072]{3,2,1,0:T(8,128)(2,1)} %bitcast.101), calls=%async_computation.2 | async-start | bytes 4718592 | tf_op jit(solution)/shard_map/all_to_all | solution.py:80
  102.5 3.2 copy-start.2
  122.4 3.2 copy-start.2
  142.3 3.2 copy-start.2
  162.2 3.2 copy-start.2
  182.2 3.2 copy-start.2
  202.1 3.2 copy-start.2
  222.0 3.2 copy-start.2
  241.9 3.2 copy-start.2
  261.8 3.2 copy-start.2
  281.8 3.2 copy-start.2
  301.7 3.2 copy-start.2
  321.6 3.2 copy-start.2
  327.9 4.4 copy-start.6
  327.9 4.5 copy-start.9
  327.9 21.2 %all-to-all-start.3 = ((bf16[8,6,8,1536]{3,2,1,0:T(8,128)(2,1)}), bf16[8,6,8,1536]{3,2,1,0:T(8,128)(2,1)}, u32[]{:S(2)}, u32[]{:S(2)}) async-start(bf16[8,6,8,1536]{3,2,1,0:T(8,128)(2,1)} %bitcast.12), calls=%async_computation.3 | async-start | bytes 2359296 | tf_op jit(solution)/shard_map/all_to_all | solution.py:140
  332.3 46.6 %all-gather.4.cloned.1.call-start = ((), (), s32[]{:S(2)}) async-start(), calls=%async_computation.5 | async-start | bytes 1327104 | tf_op jit(solution)/shard_map/all_gather | solution.py:143
  355.3 143.0 %all-gather.6.cloned.1.call-start = ((), (), s32[]{:S(2)}) async-start(), calls=%async_computation.7 | async-start | bytes 7864320 | tf_op jit(solution)/shard_map/all_gather | solution.py:146
  382.8 189.4 %reduce-scatter.2.cloned.1.call-start = ((), (), s32[]{:S(2)}) async-start(), calls=%async_computation.6 | async-start | bytes 2654208 | tf_op jit(solution)/shard_map/reduce_scatter | solution.py:161
  518.9 7.8 %copy-start.1 = (f32[384]{0:T(512)}, f32[384]{0:T(512)S(1)}, u32[]{:S(2)}) copy-start(f32[384]{0:T(512)S(1)} %fusion.33) | copy-start | bytes 4612
  (4 other events, 3.8 us)
Sparse Core Ops, SparseCore 0:
  355.4 23.4 all-gather.3
  382.9 115.3 all-gather.5
  533.3 38.8 reduce-scatter.1
